TPU v7x, 32 devices: a whole 2x2x4 slice. The times are simulated.
32 devices in a mesh: pool: 16 (over z, x, core), exp: 2 (over y).
Axes of the slice: x: 2, y: 2, z: 4, core: 2. Of those that a mesh axis runs over, the one named last changes fastest.
Arguments:
- tokens: bfloat16 [256, 1024], P('pool'), as said below
- block_table: int32 [256, 128], replicated, may hold values from -1 to 2303, as said below
- lengths: int32 [256], replicated, may hold values from 1 to 16384, as said below
- k_cache: bfloat16 [2048, 128, 512], P('pool', None, 'exp'), as said below
- v_cache: bfloat16 [2048, 128, 512], P('pool', None, 'exp'), may hold values from -9 to 9
- hidden_store: bfloat16 [256, 128, 1024], P('pool'), may hold values from -6 to 6
- norm_attn: bfloat16 [1024], replicated, may hold values from 0.5 to 1.5
- w_query: bfloat16 [1024, 1024], P(None, 'exp'), as said below
- w_key: bfloat16 [1024, 512], P(None, 'exp'), may hold values from -0.1875 to 0.1875
- w_value: bfloat16 [1024, 512], P(None, 'exp'), may hold values from -0.1875 to 0.1875
- w_out: bfloat16 [1024, 1024], P('exp'), may hold values from -0.1875 to 0.1875
- norm_moe: bfloat16 [1024], replicated, may hold values from 0.5 to 1.5
- expert_ids: int32 [256, 8], P('pool'), may hold values from 0 to 15, all different within a row; in each aligned block of 16 rows (0 to 15, 16 to 31, ...) at most 16 rows name the same one
- gate_weights: float32 [256, 8], P('pool'), may hold values from 0.1 to 1
- w_gate: bfloat16 [16, 1024, 512], P('pool'), may hold values from -0.1875 to 0.1875
- w_up: bfloat16 [16, 1024, 512], P('pool'), may hold values from -0.1875 to 0.1875
- w_down: bfloat16 [16, 512, 1024], P('pool'), may hold values from -0.25 to 0.25
Outputs:
- layer_out: bfloat16 [256, 1024], P('pool', 'exp')
Inputs may be any that keep to these rules, and one draw needn't show every extreme that they name: `block_table`: every block number 0 to 2303 stands exactly once in the table; a request's blocks fill the start of its row and -1 fills the rest; each request has 1 to 128 blocks and some request has exactly 128. `lengths`: A request with n blocks has a length above (n - 1) * 128 and at most n * 128; some request has the length 16384. `expert_ids`: in the rows of one pool index no expert is named by more than 16 rows. `tokens`: entries lie within -8 to 8. `k_cache`: entries lie within -8 to 8. `w_query`: entries are of magnitude below 7 / sqrt(1024).
All inputs are finite; a program needn't handle non-finite values.
Results may differ from a plain program's by a relative error of at most 0.009.
Values may be sent and summed in bfloat16 or wider, within the bound.
A program may use at most 128 MiB of HBM per device.

v0:
```python
import jax
import jax.numpy as jnp
from jax import lax
from jax.sharding import PartitionSpec as P

HEAD_SIZE = 64


NEG_FILL = -1e30
EPSILON = 1e-05
SCORE_SCALE = 0.125
HIGHEST = lax.Precision.HIGHEST


def merged(value, axis, join):
    pieces = jax.tree.map(lambda part: lax.all_gather(part, axis), value)
    head = jax.tree.map(lambda part: part[0], pieces)
    tail = jax.tree.map(lambda part: part[1:], pieces)
    so_far, _ = lax.scan(lambda so_far, piece: (join(so_far, piece), None), head, tail)
    return so_far


def rms_scale(row_vals, gain_row):
    mean_sq = jnp.mean(row_vals * row_vals, axis=-1, keepdims=True)
    return row_vals * lax.rsqrt(mean_sq + EPSILON) * gain_row


def merge_pair(first, second):
    top_a, sum_a, out_a = first
    top_b, sum_b, out_b = second
    row_top = jnp.maximum(top_a, top_b)
    weight_a = jnp.exp(top_a - row_top)
    weight_b = jnp.exp(top_b - row_top)
    spread = out_a.shape[-1] // top_a.shape[-1]
    merged_out = out_a * jnp.repeat(weight_a, spread, axis=-1) + out_b * jnp.repeat(
        weight_b, spread, axis=-1
    )
    return (row_top, sum_a * weight_a + sum_b * weight_b, merged_out)


def on_device(
    tokens,
    block_table,
    lengths,
    k_cache,
    v_cache,
    hidden_store,
    norm_attn,
    w_query,
    w_key,
    w_value,
    w_out,
    norm_moe,
    expert_ids,
    gate_weights,
    w_gate,
    w_up,
    w_down,
):
    pool_count = lax.axis_size("pool")
    exp_count = lax.axis_size("exp")
    pool_index = lax.axis_index("pool")
    exp_index = lax.axis_index("exp")
    req_dev = tokens.shape[0]
    model_width = tokens.shape[1]
    quarter = model_width // exp_count
    x_rows = tokens.astype(jnp.float32)
    normed = rms_scale(x_rows, norm_attn.astype(jnp.float32)).astype(jnp.bfloat16)
    queries = jnp.dot(normed, w_query, preferred_element_type=jnp.float32).astype(jnp.bfloat16)
    all_queries = lax.all_gather(queries, "pool", axis=0, tiled=True)
    stored_rows = hidden_store.reshape(-1, model_width)
    stored_shape = (hidden_store.shape[0], hidden_store.shape[1], w_key.shape[1])
    key_new = (
        jnp.dot(stored_rows, w_key, preferred_element_type=jnp.float32)
        .astype(jnp.bfloat16)
        .reshape(stored_shape)
    )
    value_new = (
        jnp.dot(stored_rows, w_value, preferred_element_type=jnp.float32)
        .astype(jnp.bfloat16)
        .reshape(stored_shape)
    )
    keys_here = jnp.concatenate([k_cache, key_new], axis=0)
    values_here = jnp.concatenate([v_cache, value_new], axis=0)
    slot_count, page_len, key_width = keys_here.shape
    query_width = queries.shape[1]
    kv_groups = key_width // HEAD_SIZE
    per_group = query_width // key_width
    head_count = query_width // HEAD_SIZE
    requests = block_table.shape[0]
    list_len = block_table.shape[1]
    flat_ids = block_table.reshape(-1)
    entry_index = jnp.arange(requests * list_len, dtype=jnp.int32)
    global_slot = pool_index * slot_count + jnp.arange(slot_count, dtype=jnp.int32)
    found_entry = jnp.sum(
        jnp.where(flat_ids[None, :] == global_slot[:, None], entry_index[None, :], 0), axis=1
    )
    slot_req = found_entry // list_len
    slot_block = found_entry % list_len
    member = slot_req[:, None] == jnp.arange(requests, dtype=jnp.int32)[None, :]
    member_low = member.astype(jnp.bfloat16)
    slot_queries = jnp.dot(member_low, all_queries, preferred_element_type=jnp.float32).astype(
        jnp.bfloat16
    )
    slot_length = jnp.sum(jnp.where(member, lengths[None, :], 0), axis=1)
    q_grouped = slot_queries.reshape(slot_count, kv_groups, per_group, HEAD_SIZE)
    k_grouped = keys_here.reshape(slot_count, page_len, kv_groups, HEAD_SIZE)
    v_grouped = values_here.reshape(slot_count, page_len, kv_groups, HEAD_SIZE)
    scores = (
        jnp.einsum("sgqd,stgd->sgqt", q_grouped, k_grouped, preferred_element_type=jnp.float32)
        * SCORE_SCALE
    )
    positions = slot_block[:, None] * page_len + jnp.arange(page_len, dtype=jnp.int32)[None, :]
    is_valid = (positions < slot_length[:, None])[:, None, None, :]
    masked = jnp.where(is_valid, scores, NEG_FILL)
    block_top = jnp.max(masked, axis=-1)
    weights = jnp.where(is_valid, jnp.exp(masked - block_top[..., None]), 0.0)
    block_sum = jnp.sum(weights, axis=-1)
    block_out = jnp.einsum(
        "sgqt,stgd->sgqd",
        weights.astype(jnp.bfloat16),
        v_grouped,
        preferred_element_type=jnp.float32,
    )
    slot_top = block_top.reshape(slot_count, head_count)
    slot_sum = block_sum.reshape(slot_count, head_count)
    slot_out = block_out.reshape(slot_count, query_width)
    local_top = jnp.max(jnp.where(member[:, :, None], slot_top[:, None, :], NEG_FILL), axis=0)
    own_top = jnp.max(jnp.where(member[:, :, None], local_top[None, :, :], NEG_FILL), axis=1)
    factor = jnp.exp(slot_top - own_top)
    one_hot = member.astype(jnp.float32)
    local_sum = jnp.einsum("sr,sh->rh", one_hot, slot_sum * factor, precision=HIGHEST)
    local_out = jnp.einsum(
        "sr,sc->rc", one_hot, slot_out * jnp.repeat(factor, HEAD_SIZE, axis=1), precision=HIGHEST
    )
    all_top, all_sum, all_out = merged((local_top, local_sum, local_out), "pool", merge_pair)
    row_start = pool_index * req_dev
    total_sum = lax.dynamic_slice_in_dim(all_sum, row_start, req_dev, 0)
    accum = lax.dynamic_slice_in_dim(all_out, row_start, req_dev, 0)
    attended = (accum / jnp.repeat(total_sum, HEAD_SIZE, axis=-1)).astype(jnp.bfloat16)
    projected = lax.psum(jnp.dot(attended, w_out, preferred_element_type=jnp.float32), "exp")
    mixed = x_rows + projected
    normed_moe = rms_scale(mixed, norm_moe.astype(jnp.float32)).astype(jnp.bfloat16)
    top_count = expert_ids.shape[1]
    capacity = min(req_dev, 2 * ((req_dev * top_count + pool_count - 1) // pool_count))
    route_flat = expert_ids.reshape(-1)
    expert_hit = (route_flat[:, None] == jnp.arange(pool_count, dtype=jnp.int32)[None, :]).astype(
        jnp.int32
    )
    slot_rank = jnp.sum(jnp.cumsum(expert_hit, axis=0) * expert_hit, axis=1) - 1
    slot_pos = route_flat * capacity + slot_rank
    placed = (
        slot_pos[:, None] == jnp.arange(pool_count * capacity, dtype=jnp.int32)[None, :]
    ).astype(jnp.float32)
    placed = placed.reshape(req_dev, top_count, pool_count * capacity)
    send_map = jnp.sum(placed, axis=1).astype(jnp.bfloat16)
    combine_map = jnp.einsum("tk,tkc->tc", gate_weights, placed, precision=HIGHEST)
    outgoing = jnp.einsum("tc,td->cd", send_map, normed_moe, preferred_element_type=jnp.float32)
    outgoing = outgoing.astype(jnp.bfloat16).reshape(pool_count, capacity, model_width)
    arrived = lax.all_to_all(outgoing, "pool", split_axis=0, concat_axis=0, tiled=True)
    sources = arrived.shape[0]
    slots_here = arrived.shape[1]
    row_block = arrived.reshape(-1, model_width)
    gate_act = jnp.dot(row_block, w_gate[0], preferred_element_type=jnp.float32)
    up_act = jnp.dot(row_block, w_up[0], preferred_element_type=jnp.float32)
    hidden = (jax.nn.silu(gate_act) * up_act).astype(jnp.bfloat16)
    expert_low = jnp.dot(hidden, w_down[0], preferred_element_type=jnp.float32).astype(jnp.bfloat16)
    expert_low = expert_low.reshape(sources, slots_here, model_width)
    expert_out = lax.dynamic_slice_in_dim(expert_low, exp_index * quarter, quarter, 2)
    returned = lax.all_to_all(expert_out, "pool", split_axis=0, concat_axis=0, tiled=True)
    moe_share = jnp.dot(
        combine_map,
        returned.reshape(pool_count * capacity, quarter).astype(jnp.float32),
        precision=HIGHEST,
    )
    mixed_share = lax.dynamic_slice_in_dim(mixed, exp_index * quarter, quarter, 1)
    return (mixed_share + moe_share).astype(jnp.bfloat16)


def solution(mesh):
    placed = (
        P("pool", None),
        P(),
        P(),
        P("pool", None, "exp"),
        P("pool", None, "exp"),
        P("pool", None, None),
        P(),
        P(None, "exp"),
        P(None, "exp"),
        P(None, "exp"),
        P("exp", None),
        P(),
        P("pool", None),
        P("pool", None),
        P("pool", None, None),
        P("pool", None, None),
        P("pool", None, None),
    )
    return jax.shard_map(
        on_device, mesh=mesh, in_specs=placed, out_specs=P("pool", "exp"), check_vma=False
    )
```

profile of v0, /device:TPU:0, one launch (start us, length us, event | category | flops | bytes accessed | tf_op | source)
XLA Modules:
  0.0 276.1 jit_solution(12098107966719097078)
XLA Ops:
  8.2 1.5 convolution_convert_fusion.5
  9.7 23.8 %all_gather.21 = bf16[256,512]{1,0:T(8,128)(2,1)S(1)} all-gather(bf16[16,512]{1,0:T(8,128)(2,1)S(1)} %convolution_convert_fusion.5), channel_id=1, replica_groups=mesh['pool'=16,'exp'=2] {'pool'}, dimensions={0}, use_global_device_ids=true | all-gather | bytes 278528 | tf_op jit(solution)/shard_map/all_gather | solution.py:70
  33.5 3.6 %select_reduce_fusion = s32[144]{0:T(256)S(1)} fusion(s32[32768]{0:T(1024)} %bitcast.85, s32[144]{0:T(256)S(1)} %iota_add_fusion), kind=kLoop, calls=%fused_computation.10 | loop fusion | flops 14155632 | bytes 132224 | tf_op jit(solution)/shard_map/reduce_sum | solution.py:95
  38.3 4.5 %convolution_convert_fusion.1 = bf16[2048,256]{1,0:T(8,128)(2,1)} fusion(bf16[2048,1024]{1,0:T(8,128)(2,1)} %bitcast.87, bf16[1024,256]{1,0:T(8,128)(2,1)} %param.27), kind=kOutput, calls=%fused_computation.20 | convolution fusion | flops 1074266112 | bytes 5767168 | tf_op jit(solution)/shard_map/dot_general | solution.py:74
  42.9 3.3 %reshape.209 = bf16[16,128,4,64]{3,2,1,0:T(4,128)(2,1)S(1)} reshape(bf16[2048,256]{1,0:T(8,128)(2,1)} %convolution_convert_fusion.1) | data formatting | bytes 2097152 | tf_op jit(solution)/shard_map/concatenate | solution.py:83
  46.2 2.2 copy.74
  48.4 12.0 %copy.72 = bf16[128,128,256]{1,2,0:T(8,128)(2,1)} copy(bf16[128,128,256]{2,1,0:T(8,128)(2,1)} %param.22) | data formatting | bytes 16777216 | tf_op args[3]
  60.8 5.9 %fusion.60 = (f32[144,4,2]{2,1,0:T(4,128)S(1)}, f32[144,4,2,128]{3,2,1,0:T(2,128)}) fusion(bf16[144,4,2,64]{3,2,1,0:T(2,128)(2,1)S(1)} %copy-done.5, bf16[16,128,4,64]{1,3,2,0:T(8,128)(2,1)S(1)} %copy-done.1, bf16[128,128,4,64]{1,3,2,0:T(8,128)(2,1)} %bitcast.77, pred[144,128]{1,0:T(8,128)(4,1)S(1)} %add_compare_fusion), kind=kOutput, calls=%fused_computation.100 | convolution fusion | flops 24034176 | bytes 10197504 | tf_op jit(solution)/shard_map/sgqd,stgd->sgqt/dot_general | solution.py:110
  67.6 4.4 %convolution_convert_fusion = bf16[2048,256]{1,0:T(8,128)(2,1)} fusion(bf16[2048,1024]{1,0:T(8,128)(2,1)} %bitcast.88, bf16[1024,256]{1,0:T(8,128)(2,1)S(1)} %copy-done.10), kind=kOutput, calls=%fused_computation.19 | convolution fusion | flops 1074266112 | bytes 5767168 | tf_op jit(solution)/shard_map/dot_general | solution.py:79
  72.0 3.3 %reshape.210 = bf16[16,128,4,64]{3,2,1,0:T(4,128)(2,1)S(1)} reshape(bf16[2048,256]{1,0:T(8,128)(2,1)} %convolution_convert_fusion) | data formatting | bytes 2097152 | tf_op jit(solution)/shard_map/concatenate | solution.py:84
  75.4 2.2 copy.81
  77.5 12.0 %copy.79 = bf16[128,128,256]{1,2,0:T(8,128)(2,1)} copy(bf16[128,128,256]{2,1,0:T(8,128)(2,1)} %param.23) | data formatting | bytes 16777216 | tf_op args[4]
  89.6 8.2 %fusion.7 = f32[144,4,2,64]{3,2,1,0:T(2,128)} fusion(bf16[16,128,4,64]{1,3,2,0:T(8,128)(2,1)S(1)} %copy-done.2, bf16[128,128,4,64]{1,3,2,0:T(8,128)(2,1)} %bitcast.78, f32[144,4,2,128]{3,2,1,0:T(2,128)S(1)} %copy-done.3, pred[144,128]{1,0:T(8,128)(4,1)S(1)} %add_compare_fusion, f32[144,4,2]{2,1,0:T(4,128)S(1)} %get-tuple-element.95), kind=kOutput, calls=%fused_computation.15 | convolution fusion | flops 24035328 | bytes 10344960 | tf_op jit(solution)/shard_map/sgqt,stgd->sgqd/dot_general | solution.py:119
  97.8 1.6 reshape.188
  99.9 1.4 fusion.29
  101.4 18.3 %all-gather = f32[4096,8]{0,1:T(8,128)S(1)} all-gather(f32[256,8]{0,1:T(8,128)S(1)} %select_reduce_fusion.2), channel_id=2, replica_groups=mesh['pool'=16,'exp'=2] {'pool'}, dimensions={0}, use_global_device_ids=true | all-gather | bytes 139264 | tf_op jit(solution)/shard_map/all_gather | solution.py:16
  119.7 1.5 fusion.51
  121.6 19.7 %all-gather.1 = f32[4096,8]{0,1:T(8,128)S(1)} all-gather(f32[256,8]{0,1:T(8,128)S(1)} %fusion.34), channel_id=3, replica_groups=mesh['pool'=16,'exp'=2] {'pool'}, dimensions={0}, use_global_device_ids=true | all-gather | bytes 139264 | tf_op jit(solution)/shard_map/all_gather | solution.py:16
  142.1 32.2 %all-gather.5.cloned.1.call-done = f32[4096,512]{1,0:T(8,128)} async-done(((f32[256,512]{1,0:T(8,128)}), f32[4096,512]{1,0:T(8,128)}) %all-gather.5.cloned.1.call-update) | async-done | bytes 8388624 | tf_op jit(solution)/shard_map/all_gather | solution.py:16
  175.6 7.3 %slice.35 = f32[3840,512]{1,0:T(8,128)} slice(f32[4096,512]{1,0:T(8,128)} %all-gather.5.cloned.1.call-done), slice={[256:4096], [0:512]} | slice | bytes 15728640 | tf_op jit(solution)/shard_map/slice | solution.py:18
  182.9 23.1 %while.14 = (s32[]{:T(128)}, f32[256,8]{0,1:T(8,128)S(1)}, f32[256,8]{0,1:T(8,128)S(1)}, f32[256,512]{0,1:T(8,128)S(1)}, f32[15,256,8]{1,2,0:T(8,128)S(1)}, /*in...) while((s32[]{:T(128)}, f32[256,8]{0,1:T(8,128)S(1)}, f32[256,8]{0,1:T(8,128)S(1)}, ...), condition=%wide.region_8.9_spmd, body=%wide.region_7.8_spmd.sunk | while | flops 405506 | bytes 3752037 | solution.py:19
  186.0 1.1 constant_dynamic-slice_fusion.4
  187.5 1.1 constant_dynamic-slice_fusion.4
  206.2 2.1 fusion.61
  208.5 19.2 %all-reduce.2.cloned.1.call-done = f32[16,1024]{1,0:T(8,128)} async-done(((f32[16,1024]{1,0:T(8,128)}), f32[16,1024]{1,0:T(8,128)}) %all-reduce.2.cloned.1.call-update) | async-done | bytes 65552 | tf_op jit(solution)/shard_map/psum | solution.py:141
  228.7 1.1 convolution_convert_fusion.3
  229.8 5.6 %all-to-all-start = ((bf16[16,16,1024]{2,1,0:T(8,128)(2,1)}), bf16[16,16,1024]{2,1,0:T(8,128)(2,1)S(1)}, u32[]{:S(2)}, u32[]{:S(2)}) async-start(bf16[16,16,1024]{2,1,0:T(8,128)(2,1)} %bitcast.15), calls=%async_computation | async-start | bytes 1048576 | tf_op jit(solution)/shard_map/all_to_all | solution.py:160
  235.4 14.5 %all-to-all-done = bf16[16,16,1024]{2,1,0:T(8,128)(2,1)S(1)} async-done(((bf16[16,16,1024]{2,1,0:T(8,128)(2,1)}), bf16[16,16,1024]{2,1,0:T(8,128)(2,1)S(1)}, u32[]{:S(2)}, u32[]{:S(2)}) %all-to-all-start) | async-done | bytes 524320 | tf_op jit(solution)/shard_map/all_to_all | solution.py:160
  249.9 1.7 fusion.19
  251.6 2.0 convolution_convert_fusion.2
  254.3 4.1 %all-to-all-start.1 = ((bf16[16,16,512]{2,1,0:T(8,128)(2,1)}), bf16[16,16,512]{2,1,0:T(8,128)(2,1)S(1)}, u32[]{:S(2)}, u32[]{:S(2)}) async-start(bf16[16,16,512]{2,1,0:T(8,128)(2,1)} %constant_dynamic-slice_fusion.2), calls=%async_computation.1 | async-start | bytes 524288 | tf_op jit(solution)/shard_map/all_to_all | solution.py:170
  258.8 9.7 %all-to-all-done.1 = bf16[16,16,512]{2,1,0:T(8,128)(2,1)S(1)} async-done(((bf16[16,16,512]{2,1,0:T(8,128)(2,1)}), bf16[16,16,512]{2,1,0:T(8,128)(2,1)S(1)}, u32[]{:S(2)}, u32[]{:S(2)}) %all-to-all-start.1) | async-done | bytes 262176 | tf_op jit(solution)/shard_map/all_to_all | solution.py:170
  (131 shorter events, 30.7 us)
Async XLA Ops:
  6.5 245.0 %copy-start = (bf16[1,512,1024]{2,1,0:T(8,128)(2,1)S(1)}, bf16[1,512,1024]{2,1,0:T(8,128)(2,1)}, u32[]{:S(2)}) copy-start(bf16[1,512,1024]{2,1,0:T(8,128)(2,1)} %param.35) | copy-start | bytes 3145732
  6.5 167.8 %all-gather.5.cloned.1.call-start = ((), (), s32[]{:S(2)}) async-start(), calls=%async_computation.3 | async-start | bytes 8912896 | tf_op jit(solution)/shard_map/all_gather | solution.py:16
  48.4 12.0 %copy-start.9 = (s32[256]{0:T(256)S(1)}, s32[256]{0:T(256)}, u32[]{:S(2)}) copy-start(s32[256]{0:T(256)} %param.21) | copy-start | bytes 3076
  48.4 12.4 %copy-start.1 = (bf16[16,128,4,64]{1,3,2,0:T(8,128)(2,1)S(1)}, bf16[16,128,4,64]{1,3,2,0:T(8,128)(2,1)}, u32[]{:S(2)}) copy-start(bf16[16,128,4,64]{1,3,2,0:T(8,128)(2,1)} %copy.74) | copy-start | bytes 3145732
  48.4 12.4 %copy-start.5 = (bf16[144,4,2,64]{3,2,1,0:T(2,128)(2,1)S(1)}, bf16[144,4,2,64]{3,2,1,0:T(2,128)(2,1)}, u32[]{:S(2)}) copy-start(bf16[144,4,2,64]{3,2,1,0:T(2,128)(2,1)} %reshape.185) | copy-start | bytes 442372
  60.8 6.8 %copy-start.10 = (bf16[1024,256]{1,0:T(8,128)(2,1)S(1)}, bf16[1024,256]{1,0:T(8,128)(2,1)}, u32[]{:S(2)}) copy-start(bf16[1024,256]{1,0:T(8,128)(2,1)} %param.28) | copy-start | bytes 1572868
  77.5 12.1 %copy-start.2 = (bf16[16,128,4,64]{1,3,2,0:T(8,128)(2,1)S(1)}, bf16[16,128,4,64]{1,3,2,0:T(8,128)(2,1)}, u32[]{:S(2)}) copy-start(bf16[16,128,4,64]{1,3,2,0:T(8,128)(2,1)} %copy.81) | copy-start | bytes 3145732
  77.5 12.1 %copy-start.3 = (f32[144,4,2,128]{3,2,1,0:T(2,128)S(1)}, f32[144,4,2,128]{3,2,1,0:T(2,128)}, u32[]{:S(2)}) copy-start(f32[144,4,2,128]{3,2,1,0:T(2,128)} %get-tuple-element.96) | copy-start | bytes 1769476
  89.6 51.8 %copy-start.8 = (bf16[1024]{0:T(1024)(128)(2,1)S(1)}, bf16[1024]{0:T(1024)(128)(2,1)}, u32[]{:S(2)}) copy-start(bf16[1024]{0:T(1024)(128)(2,1)} %param.30) | copy-start | bytes 6148
  89.6 51.8 %copy-start.6 = (s32[16,8]{0,1:T(8,128)S(1)}, s32[16,8]{0,1:T(8,128)}, u32[]{:S(2)}) copy-start(s32[16,8]{0,1:T(8,128)} %param.31) | copy-start | bytes 1540
  101.3 126.4 %all-reduce.2.cloned.1.call-start = ((), (), s32[]{:S(2)}) async-start(), calls=%async_computation.2 | async-start | bytes 131072 | tf_op jit(solution)/shard_map/psum | solution.py:141
  182.9 44.9 %copy-start.4 = (bf16[16,1024]{1,0:T(8,128)(2,1)S(1)}, bf16[16,1024]{1,0:T(8,128)(2,1)}, u32[]{:S(2)}) copy-start(bf16[16,1024]{1,0:T(8,128)(2,1)} %param.19) | copy-start | bytes 98308
  206.0 52.4 %copy-start.7 = (f32[16,8]{0,1:T(8,128)S(1)}, f32[16,8]{0,1:T(8,128)}, u32[]{:S(2)}) copy-start(f32[16,8]{0,1:T(8,128)} %param.32) | copy-start | bytes 1540
  229.8 20.1 %all-to-all-start = ((bf16[16,16,1024]{2,1,0:T(8,128)(2,1)}), bf16[16,16,1024]{2,1,0:T(8,128)(2,1)S(1)}, u32[]{:S(2)}, u32[]{:S(2)}) async-start(bf16[16,16,1024]{2,1,0:T(8,128)(2,1)} %bitcast.15), calls=%async_computation | async-start | bytes 1048576 | tf_op jit(solution)/shard_map/all_to_all | solution.py:160
  254.3 14.2 %all-to-all-start.1 = ((bf16[16,16,512]{2,1,0:T(8,128)(2,1)}), bf16[16,16,512]{2,1,0:T(8,128)(2,1)S(1)}, u32[]{:S(2)}, u32[]{:S(2)}) async-start(bf16[16,16,512]{2,1,0:T(8,128)(2,1)} %constant_dynamic-slice_fusion.2), calls=%async_computation.1 | async-start | bytes 524288 | tf_op jit(solution)/shard_map/all_to_all | solution.py:170
Sparse Core Ops, SparseCore 0:
  101.5 72.8 all-gather.4
  208.5 19.1 all-reduce.1
where the time goes:
time: 278 us; the launch traced here: 276 us
  waiting for transfers between devices  75.6 us (27%)
  local copies, waits for them, and re-layouts  67.5 us (24%)
  blocking collectives  61.8 us (22%)
  matrix products  34.5 us (12%)
  between operations  13.7 us (5%)
  other arithmetic  12.8 us (5%)
  starting transfers between devices  9.76 us (4%)
    all_gather x2, blocking collectives, merged(): pieces = jax.tree.map(lambda part: lax.all_gather(part, axis), value)  38 us
    all_gather x1, waiting for transfers between devices, merged(): pieces = jax.tree.map(lambda part: lax.all_gather(part, axis), value)  32.2 us
    unnamed x26, local copies, waits for them, and re-layouts  24.3 us
    all_gather x1, blocking collectives, on_device(): all_queries = lax.all_gather(queries, 'pool', axis=0, tiled=True)  23.8 us
    psum x1, waiting for transfers between devices, on_device(): lax.psum(jnp.dot(attended, w_out, preferred_element_type=jnp.float32), 'e...  19.2 us
    dynamic_slice x30, local copies, waits for them, and re-layouts, merged(): lax.scan(lambda so_far, piece: (join(so_far, piece), None), head, tail)  19.2 us
    all_to_all x1, waiting for transfers between devices, on_device(): lax.all_to_all(outgoing, 'pool', split_axis=0, concat_axis=0, tiled=True)  14.5 us
    all_to_all x1, waiting for transfers between devices, on_device(): lax.all_to_all(expert_out, 'pool', split_axis=0, concat_axis=0, tiled=True)  9.7 us
  transfers between devices with their start and end apart: 4, of which 4 were waited for; matrix products, arithmetic and copies ran while one was open for 1% of the time, Pallas kernels for 0%

commit v1 on v0

v1 whole, which is shorter than its diff:
```python
import functools

import jax
import jax.numpy as jnp
from jax import lax
from jax.experimental import pallas as pl
from jax.experimental.pallas import tpu as pltpu
from jax.sharding import PartitionSpec as P

HEAD_SIZE = 64
LANES = 128
NEG_FILL = -1e30
EPSILON = 1e-05
SCORE_SCALE = 0.125
VMEM_LIMIT = 56 * 1024 * 1024
MESH = pl.DeviceIdType.MESH
F32 = jnp.float32
BF16 = jnp.bfloat16
VMEM = pl.BlockSpec(memory_space=pltpu.VMEM)


def rms_scale(row_vals, gain_row):
    mean_sq = jnp.mean(row_vals * row_vals, axis=-1, keepdims=True)
    return row_vals * lax.rsqrt(mean_sq + EPSILON) * gain_row


def iota(shape, dim):
    return lax.broadcasted_iota(jnp.int32, shape, dim)


def dot(a, b):
    return jnp.dot(a, b, preferred_element_type=F32)


def dot_bt(a, b):
    return lax.dot_general(a, b, (((1,), (1,)), ((), ())), preferred_element_type=F32)


def split_two(value):
    high = value.astype(BF16)
    return high, (value - high.astype(F32)).astype(BF16)


def swap_heads(row_vals, outer, inner):
    parts = []
    for i in range(inner):
        for o in range(outer):
            start = (o * inner + i) * HEAD_SIZE
            parts.append(row_vals[:, start : start + HEAD_SIZE])
    return jnp.concatenate(parts, axis=1)


def greet_pool(me, count, barrier):
    def body(k, carry):
        pl.semaphore_signal(
            barrier, inc=1, device_id={"pool": lax.rem(me + k, count)}, device_id_type=MESH
        )
        return carry

    lax.fori_loop(1, count, body, 0)


def push(src, dst, send, recv, target):
    return pltpu.make_async_remote_copy(
        src_ref=src, dst_ref=dst, send_sem=send, recv_sem=recv, device_id=target, device_id_type=MESH
    )


def gather_rows(buf, me, count, chip_send, chip_recv, core_send, core_recv):
    chips = count // 2
    chip, core = me // 2, lax.rem(me, 2)
    partner = chip * 2 + (1 - core)

    def to_chip(k):
        there = lax.rem(chip + k, chips) * 2 + core
        return push(buf.at[me], buf.at[me], chip_send.at[k], chip_recv.at[k], {"pool": there})

    def to_core(k):
        held = lax.rem(chip - k + chips, chips) * 2 + core
        return push(buf.at[held], buf.at[held], core_send.at[k], core_recv.at[k], {"pool": partner})

    def start(k, carry):
        to_chip(k).start()
        return carry

    def forward(k, carry):
        to_chip(k).wait_recv()
        to_core(k).start()
        return carry

    def finish_core(k, carry):
        to_core(k).wait()
        return carry

    def finish_chip(k, carry):
        to_chip(k).wait_send()
        return carry

    lax.fori_loop(1, chips, start, 0)
    to_core(0).start()
    lax.fori_loop(1, chips, forward, 0)
    lax.fori_loop(0, chips, finish_core, 0)
    lax.fori_loop(1, chips, finish_chip, 0)


def exchange(src, dst, me, count, send, recv):
    def copy(k):
        there = lax.rem(me + k, count)
        return push(src.at[there], dst.at[me], send.at[k], recv.at[k], {"pool": there})

    def start(k, carry):
        copy(k).start()
        return carry

    def finish(k, carry):
        copy(k).wait()
        return carry

    lax.fori_loop(1, count, start, 0)
    dst[me] = src[me]
    lax.fori_loop(1, count, finish, 0)


def query_kernel(count, groups, per_group, tok, gain, w_q, out, chip_s, chip_r, core_s, core_r):
    me = lax.axis_index("pool")
    barrier = pltpu.get_barrier_semaphore()
    greet_pool(me, count, barrier)
    normed = rms_scale(tok[...].astype(F32), gain[...].astype(F32)).astype(BF16)
    queries = swap_heads(dot(normed, w_q[...]), groups, per_group)
    out[me] = queries.astype(BF16)
    pl.semaphore_wait(barrier, count - 1)
    gather_rows(out, me, count, chip_s, chip_r, core_s, core_r)


def attend_kernel(
    steps, groups, per_group, queries, member, valid, k_blk, v_blk, hid, w_k, w_v, out,
    kn, vn, s_out, s_top, s_sum,
):
    step = pl.program_id(0)
    chunk, page, key_width = k_blk.shape
    heads = groups * per_group

    def attend(keys, values):
        rows = pl.ds(pl.multiple_of(step * chunk, chunk), chunk)
        q = dot(member[rows, :], queries[...])
        sub = iota((chunk, heads, key_width), 1)
        lane_group = iota((chunk, heads, key_width), 2) >> 6
        q_rows = jnp.zeros((chunk, heads, key_width), F32)
        for p in range(per_group):
            part = q[:, p * key_width : (p + 1) * key_width]
            q_rows = jnp.where(sub - p * groups == lane_group, part[:, None, :], q_rows)
        scores = lax.dot_general(
            q_rows.astype(BF16), keys, (((2,), (2,)), ((0,), (0,))), preferred_element_type=F32
        ) * SCORE_SCALE
        token = iota((chunk, heads, page), 2)
        is_valid = token < valid[rows, :][:, None, :]
        masked = jnp.where(is_valid, scores, NEG_FILL)
        top = jnp.max(masked, axis=-1, keepdims=True)
        weights = jnp.where(is_valid, jnp.exp(masked - top), 0.0)
        total = jnp.sum(weights, axis=-1, keepdims=True)
        mixed = lax.dot_general(
            weights.astype(BF16), values, (((2,), (1,)), ((0,), (0,))), preferred_element_type=F32
        )
        for p in range(per_group):
            piece = jnp.where(sub - p * groups == lane_group, mixed, 0.0)
            s_out[rows, p * key_width : (p + 1) * key_width] = jnp.sum(piece, axis=1)
        diag = iota((chunk, heads, LANES), 2) == iota((chunk, heads, LANES), 1)
        s_top[rows, :] = jnp.sum(jnp.where(diag, top, 0.0), axis=1)
        s_sum[rows, :] = jnp.sum(jnp.where(diag, total, 0.0), axis=1)

    @pl.when(step < steps - 1)
    def _():
        attend(k_blk[...], v_blk[...])

    @pl.when(step == steps - 1)
    def _():
        def project(n, carry):
            kn[n] = dot(hid[n], w_k[...]).astype(BF16)
            vn[n] = dot(hid[n], w_v[...]).astype(BF16)
            return carry

        lax.fori_loop(0, chunk, project, 0)
        attend(kn[...], vn[...])
        hits = member[...]
        requests = hits.shape[1]
        is_member = hits.astype(F32) > 0.5
        tops = s_top[...]
        row_id = iota((LANES, requests), 0)
        top_t = jnp.zeros((LANES, requests), F32)
        for h in range(heads):
            best = jnp.max(jnp.where(is_member, tops[:, h : h + 1], NEG_FILL), axis=0, keepdims=True)
            top_t = jnp.where(row_id == h, best, top_t)
        top_t = top_t.astype(BF16)
        factor = jnp.exp(tops - dot_bt(hits, top_t))
        eye = (iota((requests, requests), 0) == iota((requests, requests), 1)).astype(F32).astype(BF16)
        local_top = dot_bt(eye, top_t)
        width = heads * HEAD_SIZE
        spread = (iota((LANES, width), 1) >> 6 == iota((LANES, width), 0)).astype(F32).astype(BF16)
        f_high, f_low = split_two(factor)
        scaled = s_out[...] * (dot(f_high, spread) + dot(f_low, spread))

        def gather(value):
            high, low = split_two(value)
            dims = (((0,), (0,)), ((), ()))
            return lax.dot_general(hits, high, dims, preferred_element_type=F32) + lax.dot_general(
                hits, low, dims, preferred_element_type=F32
            )

        out[:, 0:width] = gather(scaled).astype(BF16)
        sum_high, sum_low = split_two(gather(s_sum[...] * factor))
        from_lane, to_lane = iota((LANES, LANES), 0), iota((LANES, LANES), 1)
        in_heads = from_lane < heads
        shift_high = (in_heads & (to_lane == from_lane + 8)).astype(F32).astype(BF16)
        shift_low = (in_heads & (to_lane == from_lane + 16)).astype(F32).astype(BF16)
        stats = local_top + dot(sum_high, shift_high) + dot(sum_low, shift_low)
        out[:, width : width + LANES] = stats.astype(BF16)


def layer_kernel(
    count, exp_count, groups, per_group,
    msg, tok, w_o, gain, ids, gates, w_g, w_u, w_d, out,
    parts, proj_out, proj_in, rows_in, mixed_buf, made, back,
    a_s, a_r, p_s, p_r, chip_s, chip_r, core_s, core_r, b_s, b_r,
):
    me = lax.axis_index("pool")
    col = lax.axis_index("exp")
    heads = groups * per_group
    width = heads * HEAD_SIZE
    barrier = pltpu.get_barrier_semaphore()
    greet_pool(me, count, barrier)
    for j in range(1, exp_count):
        pl.semaphore_signal(
            barrier, inc=1, device_id={"exp": lax.rem(col + j, exp_count)}, device_id_type=MESH
        )
    pl.semaphore_wait(barrier, count + exp_count - 2)

    exchange(msg, parts, me, count, a_s, a_r)
    rows = tok.shape[0]
    stats = parts[:, :, width : width + LANES].reshape(count * rows, LANES)
    lane, head = iota((LANES, width), 0), iota((LANES, width), 1) >> 6
    pick_top = (lane == head).astype(F32).astype(BF16)
    pick_sum = ((lane == head + 8) | (lane == head + 16)).astype(F32).astype(BF16)
    tops = dot(stats, pick_top).reshape(count, rows, width)
    sums = dot(stats, pick_sum).reshape(count, rows, width)
    best = jnp.max(tops, axis=0)
    factor = jnp.exp(tops - best[None])
    total = jnp.sum(factor * sums, axis=0)
    accum = jnp.sum(factor * parts[:, :, 0:width].astype(F32), axis=0)
    attended = swap_heads(accum / total, per_group, groups).astype(BF16)

    proj_out[...] = dot(attended, w_o[...])

    def to_exp(j):
        there = lax.rem(col + j, exp_count)
        return push(proj_out, proj_in.at[j], p_s.at[j], p_r.at[j], {"exp": there})

    for j in range(1, exp_count):
        to_exp(j).start()
    for j in range(1, exp_count):
        to_exp(j).wait()
    projected = proj_out[...]
    for j in range(1, exp_count):
        projected = projected + proj_in[j]
    mixed = tok[...].astype(F32) + projected
    mixed_buf[...] = mixed
    rows_in[me] = rms_scale(mixed, gain[...].astype(F32)).astype(BF16)
    gather_rows(rows_in, me, count, chip_s, chip_r, core_s, core_r)

    half = out.shape[1]
    cols = pl.ds(pl.multiple_of(col * half, half), half)
    everyone = rows_in[...].reshape(count * rows, tok.shape[1])
    gate_act = dot(everyone, w_g[...])
    up_act = dot(everyone, w_u[...])
    hidden = (gate_act / (1.0 + jnp.exp(-gate_act)) * up_act).astype(BF16)
    made[...] = dot(hidden, w_d[:, cols]).astype(BF16).reshape(count, rows, half)
    exchange(made, back, me, count, b_s, b_r)

    def combine(e, total):
        coeff = jnp.sum(jnp.where(ids[...] == e, gates[...], 0.0), axis=1, keepdims=True)
        return total + coeff * back[e].astype(F32)

    share = lax.fori_loop(0, count, combine, jnp.zeros((rows, half), F32))
    out[...] = (mixed_buf[:, cols] + share).astype(BF16)


def on_device(
    tokens, block_table, lengths, k_cache, v_cache, hidden_store, norm_attn, w_query, w_key, w_value,
    w_out, norm_moe, expert_ids, gate_weights, w_gate, w_up, w_down,
):
    count = lax.axis_size("pool")
    exp_count = lax.axis_size("exp")
    pool_index = lax.axis_index("pool")
    rows, model_width = tokens.shape
    width = w_query.shape[1]
    key_width = w_key.shape[1]
    groups = key_width // HEAD_SIZE
    per_group = width // key_width
    chips = count // 2
    dma = pltpu.SemaphoreType.DMA

    all_queries = pl.pallas_call(
        functools.partial(query_kernel, count, groups, per_group),
        out_shape=jax.ShapeDtypeStruct((count, rows, width), BF16),
        in_specs=[VMEM] * 3,
        out_specs=VMEM,
        scratch_shapes=[dma((chips,))] * 4,
        compiler_params=pltpu.CompilerParams(
            collective_id=0, has_side_effects=True, vmem_limit_bytes=VMEM_LIMIT
        ),
        name="queries",
    )(tokens, norm_attn.reshape(1, model_width), w_query)

    kept, page = k_cache.shape[0], k_cache.shape[1]
    chunk = hidden_store.shape[0]
    slot_count = kept + chunk
    requests, list_len = block_table.shape
    slots = pool_index * slot_count + jnp.arange(slot_count, dtype=jnp.int32)
    entry = jnp.arange(requests * list_len, dtype=jnp.int32)
    found = jnp.sum(
        jnp.where(block_table.reshape(-1)[None, :] == slots[:, None], entry[None, :], 0), axis=1
    )
    slot_req = found // list_len
    slot_block = found % list_len
    is_member = slot_req[:, None] == jnp.arange(requests, dtype=jnp.int32)[None, :]
    slot_length = jnp.sum(jnp.where(is_member, lengths[None, :], 0), axis=1)
    valid = jnp.broadcast_to((slot_length - slot_block * page)[:, None], (slot_count, page))

    steps = kept // chunk + 1
    whole = lambda shape: pl.BlockSpec(shape, lambda i: (0,) * len(shape))
    cache = pl.BlockSpec((chunk, page, key_width), lambda i: (jnp.minimum(i, steps - 2), 0, 0))
    message = pl.pallas_call(
        functools.partial(attend_kernel, steps, groups, per_group),
        grid=(steps,),
        out_shape=jax.ShapeDtypeStruct((requests, width + LANES), BF16),
        in_specs=[
            whole((requests, width)),
            whole((slot_count, requests)),
            whole((slot_count, page)),
            cache,
            cache,
            whole((chunk, page, model_width)),
            whole((model_width, key_width)),
            whole((model_width, key_width)),
        ],
        out_specs=whole((requests, width + LANES)),
        scratch_shapes=[
            pltpu.VMEM((chunk, page, key_width), BF16),
            pltpu.VMEM((chunk, page, key_width), BF16),
            pltpu.VMEM((slot_count, width), F32),
            pltpu.VMEM((slot_count, LANES), F32),
            pltpu.VMEM((slot_count, LANES), F32),
        ],
        compiler_params=pltpu.CompilerParams(
            dimension_semantics=("arbitrary",), vmem_limit_bytes=VMEM_LIMIT
        ),
        name="attend",
    )(
        all_queries.reshape(requests, width), is_member.astype(BF16), valid, k_cache, v_cache,
        hidden_store, w_key, w_value,
    )

    half = model_width // exp_count
    return pl.pallas_call(
        functools.partial(layer_kernel, count, exp_count, groups, per_group),
        out_shape=jax.ShapeDtypeStruct((rows, half), BF16),
        in_specs=[VMEM] * 9,
        out_specs=VMEM,
        scratch_shapes=[
            pltpu.VMEM((count, rows, width + LANES), BF16),
            pltpu.VMEM((rows, model_width), F32),
            pltpu.VMEM((exp_count, rows, model_width), F32),
            pltpu.VMEM((count, rows, model_width), BF16),
            pltpu.VMEM((rows, model_width), F32),
            pltpu.VMEM((count, rows, half), BF16),
            pltpu.VMEM((count, rows, half), BF16),
            dma((count,)), dma((count,)),
            dma((exp_count,)), dma((exp_count,)),
            dma((chips,)), dma((chips,)), dma((chips,)), dma((chips,)),
            dma((count,)), dma((count,)),
        ],
        compiler_params=pltpu.CompilerParams(
            collective_id=1, has_side_effects=True, vmem_limit_bytes=VMEM_LIMIT
        ),
        name="layer",
    )(
        message.reshape(count, rows, width + LANES), tokens, w_out, norm_moe.reshape(1, model_width),
        expert_ids, gate_weights, w_gate[0], w_up[0], w_down[0],
    )


def solution(mesh):
    placed = (
        P("pool", None),
        P(),
        P(),
        P("pool", None, "exp"),
        P("pool", None, "exp"),
        P("pool", None, None),
        P(),
        P(None, "exp"),
        P(None, "exp"),
        P(None, "exp"),
        P("exp", None),
        P(),
        P("pool", None),
        P("pool", None),
        P("pool", None, None),
        P("pool", None, None),
        P("pool", None, None),
    )
    return jax.shard_map(
        on_device, mesh=mesh, in_specs=placed, out_specs=P("pool", "exp"), check_vma=False
    )
```

time: 278 us -> 80 us (0.29)
  waiting for transfers between devices: 75.6 us -> 0 us
  Pallas kernels: 0 us -> 68.4 us
  local copies, waits for them, and re-layouts: 67.5 us -> 5.27 us
  blocking collectives: 61.8 us -> 0 us
  matrix products: 34.5 us -> 0 us
  between operations: 13.7 us -> 0.05 us
  starting transfers between devices: 9.76 us -> 0 us
  other arithmetic: 12.8 us -> 5.19 us
    pallas_call x0 -> x3, Pallas kernels: none -> 68.4 us  [the longest x1 36.4 us: on_device(): pl.pallas_call(functools.partial(layer_kernel, count, exp_count, groups,...]
    all_gather x3 -> x0, blocking collectives: 61.8 us -> none  [the longest x2 38 us: merged(): pieces = jax.tree.map(lambda part: lax.all_gather(part, axis), value)]
    dot_general x14 -> x0, matrix products: 34.5 us -> none  [the longest x1 8.23 us: on_device(): jnp.einsum('sgqt,stgd->sgqd', weights.astype(jnp.bfloat16), v_grouped, pr...]
    all_gather x1 -> x0, waiting for transfers between devices: 32.2 us -> none  [merged(): pieces = jax.tree.map(lambda part: lax.all_gather(part, axis), value)]
    all_to_all x2 -> x0, waiting for transfers between devices: 24.2 us -> none  [the longest x1 14.5 us: on_device(): lax.all_to_all(outgoing, 'pool', split_axis=0, concat_axis=0, tiled=True)]
    unnamed x26 -> x9, local copies, waits for them, and re-layouts: 24.3 us -> 2.68 us
    dynamic_slice x32 -> x0, local copies, waits for them, and re-layouts: 20 us -> none  [the longest x30 19.2 us: merged(): lax.scan(lambda so_far, piece: (join(so_far, piece), None), head, tail)]
    psum x1 -> x0, waiting for transfers between devices: 19.2 us -> none  [on_device(): lax.psum(jnp.dot(attended, w_out, preferred_element_type=jnp.float32), 'e...]
  transfers between devices with their start and end apart: 4 -> 0, of which waited for: 4 -> 0; matrix products, arithmetic and copies ran while one was open for 1% -> 0% of each run, Pallas kernels for 0% -> 0%
where the time goes in v1:
time: 80 us; the launch traced here: 78.9 us
  Pallas kernels  68.4 us (86%)
  local copies, waits for them, and re-layouts  5.27 us (7%)
  other arithmetic  5.19 us (6%)
    pallas_call x1, Pallas kernels, on_device(): pl.pallas_call(functools.partial(layer_kernel, count, exp_count, groups,...  36.4 us
    pallas_call x1, Pallas kernels, on_device(): pl.pallas_call(functools.partial(attend_kernel, steps, groups, per_group)...  19.5 us
    pallas_call x1, Pallas kernels, on_device(): pl.pallas_call(functools.partial(query_kernel, count, groups, per_group),...  12.5 us
    reduce_sum x1, other arithmetic, on_device(): jnp.sum(jnp.where(block_table.reshape(-1)[None, :] == slots[:, None], ent...  3.59 us
    unnamed x9, local copies, waits for them, and re-layouts  2.68 us

profile of v1, /device:TPU:0, one launch (start us, length us, event | category | flops | bytes accessed | tf_op | source)
XLA Modules:
  0.0 78.9 jit_solution(142968674647920276)
XLA Ops:
  0.0 3.6 %select_reduce_fusion = s32[144]{0:T(256)S(1)} fusion(s32[32768]{0:T(1024)} %bitcast.11, s32[144]{0:T(256)S(1)} %iota_add_fusion), kind=kLoop, calls=%fused_computation | loop fusion | flops 14155632 | bytes 132224 | tf_op jit(solution)/shard_map/reduce_sum | solution.py:319
  3.6 0.9 %select_reduce_fusion.1 = s32[144]{0:T(256)S(1)} fusion(s32[256]{0:T(256)} %param.19, s32[144]{0:T(256)S(1)} %and_select_fusion.1), kind=kLoop, calls=%fused_computation.1 | loop fusion | flops 110448 | bytes 2176 | tf_op jit(solution)/shard_map/reduce_sum | solution.py:325
  4.5 0.7 broadcast_in_dim.39.valid
  5.2 0.7 fusion.member
  5.9 1.3 %reshape.52.gain = bf16[1,1024]{1,0:T(2,128)(2,1)} reshape(bf16[1024]{0:T(1024)(128)(2,1)} %param.23) | data formatting | bytes 4096 | tf_op jit(solution)/shard_map/reshape | solution.py:311
  7.2 12.5 %queries.1 = bf16[16,16,512]{2,1,0:T(8,128)(2,1)} custom-call(bf16[16,1024]{1,0:T(8,128)(2,1)} %tok.3, bf16[1,1024]{1,0:T(2,128)(2,1)} %reshape.52.gain, bf16[1024,512]{1,0:T(8,128)(2,1)} %w_q.1), custom_call_target="tpu_custom_call" | custom-call | tf_op jit(solution)/shard_map/queries/pallas_call | solution.py:301
  19.8 0.0 copy-start
  19.8 0.0 copy-start.1
  19.8 0.0 copy-start.2
  19.8 19.5 %attend.1 = bf16[256,640]{1,0:T(8,128)(2,1)} custom-call(bf16[256,512]{1,0:T(8,128)(2,1)} %bitcast.7, bf16[144,256]{1,0:T(8,128)(2,1)} %fusion.member, s32[144,128]{1,0:T(8,128)} %broadcast_in_dim.39.valid, bf16[128,128,256]{2,1,0:T(8,128)(2,1)} %k_blk.1, bf16[128,128,256]{2,1,0:T(8,128)(2,1)} %v_blk.1, bf16[16,128,1024]{2,1,0:T(8,128)(2,1)} %hid.1, ...), custom_call_target="tpu_custom_call" | custom-call | tf_op jit(solution)/shard_map/attend/pallas_call | solution.py:331
  39.3 0.0 copy-done
  39.3 0.7 copy.20.ids
  40.0 0.0 copy-done.1
  40.0 0.7 copy.21.gates
  40.6 0.0 copy-done.2
  40.6 0.6 reshape.55.gain
  41.2 36.4 %layer.1 = bf16[16,512]{1,0:T(8,128)(2,1)} custom-call(bf16[16,16,640]{2,1,0:T(8,128)(2,1)} %bitcast.6, bf16[16,1024]{1,0:T(8,128)(2,1)} %tok.3, bf16[512,1024]{1,0:T(8,128)(2,1)} %w_o.1, bf16[1,1024]{1,0:T(2,128)(2,1)} %reshape.55.gain, s32[16,8]{1,0:T(8,128)} %copy.20.ids, f32[16,8]{1,0:T(8,128)} %copy.21.gates, bf16[1024,512]{1,0:T(8,128)(2,1)} %bitcast.8, ...), custom_call_target="tpu_custom_call" | custom-call | tf_op jit(solution)/shard_map/layer/pallas_call | solution.py:363
  77.6 1.3 %copy.23 = bf16[16,512]{1,0:T(8,128)(2,1)} copy(bf16[16,512]{1,0:T(8,128)(2,1)} %layer.1) | data formatting | bytes 32768
  (3 shorter events, 0.0 us)
Async XLA Ops:
  19.8 19.5 %copy-start = (s32[16,8]{0,1:T(8,128)S(1)}, s32[16,8]{0,1:T(8,128)}, u32[]{:S(2)}) copy-start(s32[16,8]{0,1:T(8,128)} %param.29) | copy-start | bytes 1540
  19.8 20.2 %copy-start.1 = (f32[16,8]{0,1:T(8,128)S(1)}, f32[16,8]{0,1:T(8,128)}, u32[]{:S(2)}) copy-start(f32[16,8]{0,1:T(8,128)} %param.30) | copy-start | bytes 1540
  19.8 20.8 %copy-start.2 = (bf16[1024]{0:T(1024)(128)(2,1)S(1)}, bf16[1024]{0:T(1024)(128)(2,1)}, u32[]{:S(2)}) copy-start(bf16[1024]{0:T(1024)(128)(2,1)} %param.28) | copy-start | bytes 6148

commit v2 on v1

v2 whole, which is shorter than its diff:
```python
import functools

import jax
import jax.numpy as jnp
from jax import lax
from jax.experimental import pallas as pl
from jax.experimental.pallas import tpu as pltpu
from jax.sharding import PartitionSpec as P

HEAD_SIZE = 64
LANES = 128
NEG_FILL = -1e30
EPSILON = 1e-05
SCORE_SCALE = 0.125
VMEM_LIMIT = 56 * 1024 * 1024
MESH = pl.DeviceIdType.MESH
F32 = jnp.float32
BF16 = jnp.bfloat16
VMEM = pl.BlockSpec(memory_space=pltpu.VMEM)


def rms_scale(row_vals, gain_row):
    mean_sq = jnp.mean(row_vals * row_vals, axis=-1, keepdims=True)
    return row_vals * lax.rsqrt(mean_sq + EPSILON) * gain_row


def iota(shape, dim):
    return lax.broadcasted_iota(jnp.int32, shape, dim)


def dot(a, b):
    return jnp.dot(a, b, preferred_element_type=F32)


def dot_bt(a, b):
    return lax.dot_general(a, b, (((1,), (1,)), ((), ())), preferred_element_type=F32)


def split_two(value):
    high = value.astype(BF16)
    return high, (value - high.astype(F32)).astype(BF16)


def swap_heads(row_vals, outer, inner):
    parts = []
    for i in range(inner):
        for o in range(outer):
            start = (o * inner + i) * HEAD_SIZE
            parts.append(row_vals[:, start : start + HEAD_SIZE])
    return jnp.concatenate(parts, axis=1)


def greet_pool(me, count, barrier):
    def body(k, carry):
        pl.semaphore_signal(
            barrier, inc=1, device_id={"pool": lax.rem(me + k, count)}, device_id_type=MESH
        )
        return carry

    lax.fori_loop(1, count, body, 0)


def push(src, dst, send, recv, target):
    return pltpu.make_async_remote_copy(
        src_ref=src, dst_ref=dst, send_sem=send, recv_sem=recv, device_id=target, device_id_type=MESH
    )


def gather_rows(buf, me, count, chip_send, chip_recv, core_send, core_recv, early=None, late=None):
    chips = count // 2
    chip, core = me // 2, lax.rem(me, 2)
    partner = chip * 2 + (1 - core)

    def to_chip(k):
        there = lax.rem(chip + k, chips) * 2 + core
        return push(buf.at[me], buf.at[me], chip_send.at[k], chip_recv.at[k], {"pool": there})

    def to_core(k):
        held = lax.rem(chip - k + chips, chips) * 2 + core
        return push(buf.at[held], buf.at[held], core_send.at[k], core_recv.at[k], {"pool": partner})

    def start(k, carry):
        to_chip(k).start()
        return carry

    def forward(k, carry):
        to_chip(k).wait_recv()
        to_core(k).start()
        return carry

    def finish_core(k, carry):
        to_core(k).wait()
        return carry

    def finish_chip(k, carry):
        to_chip(k).wait_send()
        return carry

    lax.fori_loop(1, chips, start, 0)
    to_core(0).start()
    if early is not None:
        early()
    lax.fori_loop(1, chips, forward, 0)
    if late is not None:
        late()
    lax.fori_loop(0, chips, finish_core, 0)
    lax.fori_loop(1, chips, finish_chip, 0)


def exchange(src, dst, me, count, send, recv):
    def copy(k):
        there = lax.rem(me + k, count)
        return push(src.at[there], dst.at[me], send.at[k], recv.at[k], {"pool": there})

    def start(k, carry):
        copy(k).start()
        return carry

    def finish(k, carry):
        copy(k).wait()
        return carry

    lax.fori_loop(1, count, start, 0)
    dst[me] = src[me]
    lax.fori_loop(1, count, finish, 0)


def layer_kernel(
    count, exp_count, groups, per_group,
    tok, gain_a, gain_m, table, lengths, ids, gates, w_q_h, w_k_h, w_v_h, hid_h, k_h, v_h,
    w_o_h, w_g_h, w_u_h, w_d_h, out,
    w_q, w_k, w_v, hid, keys, values, w_o, w_g, w_u, w_d,
    queries, code, valid, s_out, s_top, s_sum,
    msg, parts, proj_out, proj_in, rows_in, mixed_buf, made, back,
    load, q_cs, q_cr, q_ps, q_pr,
    a_s, a_r, p_s, p_r, chip_s, chip_r, core_s, core_r, b_s, b_r,
):
    me = lax.axis_index("pool")
    col = lax.axis_index("exp")
    heads = groups * per_group
    width = heads * HEAD_SIZE
    rows, model_width = tok.shape
    slot_count, page, key_width = keys.shape
    kept = k_h.shape[0]
    fresh = slot_count - kept
    requests = count * rows
    barrier = pltpu.get_barrier_semaphore()
    greet_pool(me, count, barrier)
    for j in range(1, exp_count):
        pl.semaphore_signal(
            barrier, inc=1, device_id={"exp": lax.rem(col + j, exp_count)}, device_id_type=MESH
        )

    moves = [(w_q_h, w_q), (w_k_h, w_k), (w_v_h, w_v), (hid_h, hid)]
    span = kept // 4
    for n in range(4):
        part = pl.ds(n * span, span)
        moves.append((k_h.at[part], keys.at[part]))
        moves.append((v_h.at[part], values.at[part]))
    moves += [(w_o_h, w_o), (w_g_h, w_g), (w_u_h, w_u), (w_d_h, w_d)]
    loads = [pltpu.make_async_copy(s, d, load.at[n]) for n, (s, d) in enumerate(moves)]
    for item in loads:
        item.start()

    normed = rms_scale(tok[...].astype(F32), gain_a[...].astype(F32)).astype(BF16)
    loads[0].wait()
    queries[me] = swap_heads(dot(normed, w_q[...]), groups, per_group).astype(BF16)
    pl.semaphore_wait(barrier, count + exp_count - 2)

    def find_slots():
        turned = table[...].T
        place = iota(turned.shape, 0) + 1
        base = me * slot_count

        def eight(n, carry):
            for i in range(8):
                hit = jnp.where(turned == base + n * 8 + i, place, 0)
                code[pl.ds(n * 8 + i, 1), :] = jnp.sum(hit, axis=0, keepdims=True)
            return carry

        lax.fori_loop(0, slot_count // 8, eight, 0)
        found = code[...]
        left = jnp.where(found > 0, lengths[...].reshape(1, requests) - (found - 1) * page, 0)
        valid[...] = jnp.broadcast_to(jnp.sum(left, axis=1, keepdims=True), valid.shape)

    def project_hidden():
        for n in range(1, 4):
            loads[n].wait()

        def one(n, carry):
            keys[kept + n] = dot(hid[n], w_k[...]).astype(BF16)
            values[kept + n] = dot(hid[n], w_v[...]).astype(BF16)
            return carry

        lax.fori_loop(0, fresh, one, 0)

    gather_rows(queries, me, count, q_cs, q_cr, q_ps, q_pr, find_slots, project_hidden)
    for n in range(4, 12):
        loads[n].wait()

    all_queries = queries[...].reshape(requests, width)
    chunk = 48 if slot_count % 48 == 0 else 16

    def attend(step, carry):
        take = pl.ds(pl.multiple_of(step * chunk, chunk), chunk)
        q = dot((code[take, :] > 0).astype(F32).astype(BF16), all_queries)
        sub = iota((chunk, heads, key_width), 1)
        lane_group = iota((chunk, heads, key_width), 2) >> 6
        q_rows = jnp.zeros((chunk, heads, key_width), F32)
        for p in range(per_group):
            part = q[:, p * key_width : (p + 1) * key_width]
            q_rows = jnp.where(sub - p * groups == lane_group, part[:, None, :], q_rows)
        scores = lax.dot_general(
            q_rows.astype(BF16), keys[take], (((2,), (2,)), ((0,), (0,))), preferred_element_type=F32
        ) * SCORE_SCALE
        token = iota((chunk, heads, page), 2)
        is_valid = token < valid[take, :][:, None, :]
        masked = jnp.where(is_valid, scores, NEG_FILL)
        top = jnp.max(masked, axis=-1, keepdims=True)
        weights = jnp.where(is_valid, jnp.exp(masked - top), 0.0)
        total = jnp.sum(weights, axis=-1, keepdims=True)
        mixed = lax.dot_general(
            weights.astype(BF16), values[take], (((2,), (1,)), ((0,), (0,))),
            preferred_element_type=F32,
        )
        for p in range(per_group):
            piece = jnp.where(sub - p * groups == lane_group, mixed, 0.0)
            s_out[take, p * key_width : (p + 1) * key_width] = jnp.sum(piece, axis=1)
        diag = iota((chunk, heads, LANES), 2) == iota((chunk, heads, LANES), 1)
        s_top[take, :] = jnp.sum(jnp.where(diag, top, 0.0), axis=1)
        s_sum[take, :] = jnp.sum(jnp.where(diag, total, 0.0), axis=1)
        return carry

    lax.fori_loop(0, slot_count // chunk, attend, 0)

    is_member = code[...] > 0
    hits = is_member.astype(F32).astype(BF16)
    tops = s_top[...]
    row_id = iota((LANES, requests), 0)
    top_t = jnp.zeros((LANES, requests), F32)
    for h in range(heads):
        best = jnp.max(jnp.where(is_member, tops[:, h : h + 1], NEG_FILL), axis=0, keepdims=True)
        top_t = jnp.where(row_id == h, best, top_t)
    top_t = top_t.astype(BF16)
    factor = jnp.exp(tops - dot_bt(hits, top_t))
    eye = (iota((requests, requests), 0) == iota((requests, requests), 1)).astype(F32).astype(BF16)
    local_top = dot_bt(eye, top_t)
    spread = (iota((LANES, width), 1) >> 6 == iota((LANES, width), 0)).astype(F32).astype(BF16)
    f_high, f_low = split_two(factor)
    scaled = s_out[...] * (dot(f_high, spread) + dot(f_low, spread))

    def by_request(value):
        high, low = split_two(value)
        dims = (((0,), (0,)), ((), ()))
        return lax.dot_general(hits, high, dims, preferred_element_type=F32) + lax.dot_general(
            hits, low, dims, preferred_element_type=F32
        )

    msg[:, :, 0:width] = by_request(scaled).astype(BF16).reshape(count, rows, width)
    sum_high, sum_low = split_two(by_request(s_sum[...] * factor))
    from_lane, to_lane = iota((LANES, LANES), 0), iota((LANES, LANES), 1)
    in_heads = from_lane < heads
    shift_high = (in_heads & (to_lane == from_lane + 8)).astype(F32).astype(BF16)
    shift_low = (in_heads & (to_lane == from_lane + 16)).astype(F32).astype(BF16)
    stats = local_top + dot(sum_high, shift_high) + dot(sum_low, shift_low)
    msg[:, :, width : width + LANES] = stats.astype(BF16).reshape(count, rows, LANES)

    exchange(msg, parts, me, count, a_s, a_r)
    stats = parts[:, :, width : width + LANES].reshape(count * rows, LANES)
    lane, head = iota((LANES, width), 0), iota((LANES, width), 1) >> 6
    pick_top = (lane == head).astype(F32).astype(BF16)
    pick_sum = ((lane == head + 8) | (lane == head + 16)).astype(F32).astype(BF16)
    tops = dot(stats, pick_top).reshape(count, rows, width)
    sums = dot(stats, pick_sum).reshape(count, rows, width)
    best = jnp.max(tops, axis=0)
    factor = jnp.exp(tops - best[None])
    total = jnp.sum(factor * sums, axis=0)
    accum = jnp.sum(factor * parts[:, :, 0:width].astype(F32), axis=0)
    attended = swap_heads(accum / total, per_group, groups).astype(BF16)

    for n in range(12, 16):
        loads[n].wait()
    proj_out[...] = dot(attended, w_o[...])

    def to_exp(j):
        there = lax.rem(col + j, exp_count)
        return push(proj_out, proj_in.at[j], p_s.at[j], p_r.at[j], {"exp": there})

    for j in range(1, exp_count):
        to_exp(j).start()
    for j in range(1, exp_count):
        to_exp(j).wait()
    projected = proj_out[...]
    for j in range(1, exp_count):
        projected = projected + proj_in[j]
    mixed = tok[...].astype(F32) + projected
    mixed_buf[...] = mixed
    rows_in[me] = rms_scale(mixed, gain_m[...].astype(F32)).astype(BF16)
    gather_rows(rows_in, me, count, chip_s, chip_r, core_s, core_r)

    half = out.shape[1]
    cols = pl.ds(pl.multiple_of(col * half, half), half)
    everyone = rows_in[...].reshape(count * rows, tok.shape[1])
    gate_act = dot(everyone, w_g[...])
    up_act = dot(everyone, w_u[...])
    hidden = (gate_act / (1.0 + jnp.exp(-gate_act)) * up_act).astype(BF16)
    made[...] = dot(hidden, w_d[:, cols]).astype(BF16).reshape(count, rows, half)
    exchange(made, back, me, count, b_s, b_r)

    def combine(e, total):
        coeff = jnp.sum(jnp.where(ids[...] == e, gates[...], 0.0), axis=1, keepdims=True)
        return total + coeff * back[e].astype(F32)

    share = lax.fori_loop(0, count, combine, jnp.zeros((rows, half), F32))
    out[...] = (mixed_buf[:, cols] + share).astype(BF16)


def on_device(
    tokens, block_table, lengths, k_cache, v_cache, hidden_store, norm_attn, w_query, w_key, w_value,
    w_out, norm_moe, expert_ids, gate_weights, w_gate, w_up, w_down,
):
    count = lax.axis_size("pool")
    exp_count = lax.axis_size("exp")
    rows, model_width = tokens.shape
    width = w_query.shape[1]
    key_width = w_key.shape[1]
    groups = key_width // HEAD_SIZE
    per_group = width // key_width
    chips = count // 2
    dma = pltpu.SemaphoreType.DMA
    page = k_cache.shape[1]
    slot_count = k_cache.shape[0] + hidden_store.shape[0]
    requests = block_table.shape[0]
    half = model_width // exp_count
    hidden_units = w_gate.shape[2]
    big = pl.BlockSpec(memory_space=pl.ANY)
    return pl.pallas_call(
        functools.partial(layer_kernel, count, exp_count, groups, per_group),
        out_shape=jax.ShapeDtypeStruct((rows, half), BF16),
        in_specs=[VMEM] * 7 + [big] * 10,
        out_specs=VMEM,
        scratch_shapes=[
            pltpu.VMEM(w_query.shape, BF16),
            pltpu.VMEM(w_key.shape, BF16),
            pltpu.VMEM(w_value.shape, BF16),
            pltpu.VMEM(hidden_store.shape, BF16),
            pltpu.VMEM((slot_count, page, key_width), BF16),
            pltpu.VMEM((slot_count, page, key_width), BF16),
            pltpu.VMEM(w_out.shape, BF16),
            pltpu.VMEM((model_width, hidden_units), BF16),
            pltpu.VMEM((model_width, hidden_units), BF16),
            pltpu.VMEM((hidden_units, model_width), BF16),
            pltpu.VMEM((count, rows, width), BF16),
            pltpu.VMEM((slot_count, requests), jnp.int32),
            pltpu.VMEM((slot_count, page), jnp.int32),
            pltpu.VMEM((slot_count, width), F32),
            pltpu.VMEM((slot_count, LANES), F32),
            pltpu.VMEM((slot_count, LANES), F32),
            pltpu.VMEM((count, rows, width + LANES), BF16),
            pltpu.VMEM((count, rows, width + LANES), BF16),
            pltpu.VMEM((rows, model_width), F32),
            pltpu.VMEM((exp_count, rows, model_width), F32),
            pltpu.VMEM((count, rows, model_width), BF16),
            pltpu.VMEM((rows, model_width), F32),
            pltpu.VMEM((count, rows, half), BF16),
            pltpu.VMEM((count, rows, half), BF16),
            dma((16,)),
            dma((chips,)), dma((chips,)), dma((chips,)), dma((chips,)),
            dma((count,)), dma((count,)),
            dma((exp_count,)), dma((exp_count,)),
            dma((chips,)), dma((chips,)), dma((chips,)), dma((chips,)),
            dma((count,)), dma((count,)),
        ],
        compiler_params=pltpu.CompilerParams(
            collective_id=0, has_side_effects=True, vmem_limit_bytes=VMEM_LIMIT
        ),
        name="layer",
    )(
        tokens, norm_attn.reshape(1, -1), norm_moe.reshape(1, -1), block_table, lengths,
        expert_ids, gate_weights, w_query, w_key, w_value, hidden_store, k_cache, v_cache,
        w_out, w_gate[0], w_up[0], w_down[0],
    )


def solution(mesh):
    placed = (
        P("pool", None),
        P(),
        P(),
        P("pool", None, "exp"),
        P("pool", None, "exp"),
        P("pool", None, None),
        P(),
        P(None, "exp"),
        P(None, "exp"),
        P(None, "exp"),
        P("exp", None),
        P(),
        P("pool", None),
        P("pool", None),
        P("pool", None, None),
        P("pool", None, None),
        P("pool", None, None),
    )
    return jax.shard_map(
        on_device, mesh=mesh, in_specs=placed, out_specs=P("pool", "exp"), check_vma=False
    )
```

time: 80 us -> 59.9 us (0.75)
  Pallas kernels: 68.4 us -> 52.3 us
  other arithmetic: 5.19 us -> 0 us
  local copies, waits for them, and re-layouts: 5.27 us -> 6.57 us
    pallas_call x2 -> x0, Pallas kernels: 32 us -> none  [the longest x1 19.5 us: on_device(): pl.pallas_call(functools.partial(attend_kernel, steps, groups, per_group)...]
    pallas_call x1, Pallas kernels: 36.4 us -> 52.3 us  [on_device(): pl.pallas_call(functools.partial(layer_kernel, count, exp_count, groups,...]
    reduce_sum x2 -> x0, other arithmetic: 4.46 us -> none  [the longest x1 3.59 us: on_device(): jnp.sum(jnp.where(block_table.reshape(-1)[None, :] == slots[:, None], ent...]
    unnamed x9 -> x3, local copies, waits for them, and re-layouts: 2.68 us -> 4.02 us
where the time goes in v2:
time: 59.9 us; the launch traced here: 58.8 us
  Pallas kernels  52.3 us (87%)
  local copies, waits for them, and re-layouts  6.57 us (11%)
    pallas_call x1, Pallas kernels, on_device(): pl.pallas_call(functools.partial(layer_kernel, count, exp_count, groups,...  52.3 us
    unnamed x3, local copies, waits for them, and re-layouts  4.02 us
    reshape x1, local copies, waits for them, and re-layouts, on_device(): norm_moe.reshape(1, -1)  1.28 us
    reshape x1, local copies, waits for them, and re-layouts, on_device(): norm_attn.reshape(1, -1)  1.27 us

profile of v2, /device:TPU:0, one launch (start us, length us, event | category | flops | bytes accessed | tf_op | source)
XLA Modules:
  0.0 58.8 jit_solution(12758903810503891337)
XLA Ops:
  0.0 1.3 %reshape.6.gain_a = bf16[1,1024]{1,0:T(2,128)(2,1)} reshape(bf16[1024]{0:T(1024)(128)(2,1)} %param.23) | data formatting | bytes 4096 | tf_op jit(solution)/shard_map/reshape | solution.py:379
  1.3 1.3 %reshape.7.gain_m = bf16[1,1024]{1,0:T(2,128)(2,1)} reshape(bf16[1024]{0:T(1024)(128)(2,1)} %param.28) | data formatting | bytes 4096 | tf_op jit(solution)/shard_map/reshape | solution.py:379
  2.5 1.4 %copy.18.ids = s32[16,8]{1,0:T(8,128)} copy(s32[16,8]{0,1:T(8,128)} %param.29) | data formatting | bytes 1024 | tf_op args[12]
  3.9 1.3 %copy.19.gates = f32[16,8]{1,0:T(8,128)} copy(f32[16,8]{0,1:T(8,128)} %param.30) | data formatting | bytes 1024 | tf_op args[13]
  5.2 52.3 %layer.1 = bf16[16,512]{1,0:T(8,128)(2,1)} custom-call(bf16[16,1024]{1,0:T(8,128)(2,1)} %tok.1, bf16[1,1024]{1,0:T(2,128)(2,1)} %reshape.6.gain_a, bf16[1,1024]{1,0:T(2,128)(2,1)} %reshape.7.gain_m, s32[256,128]{1,0:T(8,128)} %table.1, s32[256]{0:T(256)} %lengths.1, s32[16,8]{1,0:T(8,128)} %copy.18.ids, f32[16,8]{1,0:T(8,128)} %copy.19.gates, ...), custom_call_target="tpu_custom_call" | custom-call | tf_op jit(solution)/shard_map/layer/pallas_call | solution.py:337
  57.5 1.3 %copy.21 = bf16[16,512]{1,0:T(8,128)(2,1)} copy(bf16[16,512]{1,0:T(8,128)(2,1)} %layer.1) | data formatting | bytes 32768

commit v3 on v2

--- a/solution.py
+++ b/solution.py
@@ -131,7 +131,7 @@
     w_o_h, w_g_h, w_u_h, w_d_h, out,
     w_q, w_k, w_v, hid, keys, values, w_o, w_g, w_u, w_d,
     queries, code, valid, s_out, s_top, s_sum,
-    msg, parts, proj_out, proj_in, rows_in, mixed_buf, made, back,
+    msg, parts, proj_out, proj_in, rows_in, mixed_buf, made, back, coeff,
     load, q_cs, q_cr, q_ps, q_pr,
     a_s, a_r, p_s, p_r, chip_s, chip_r, core_s, core_r, b_s, b_r,
 ):
@@ -159,11 +159,12 @@
         moves.append((v_h.at[part], values.at[part]))
     moves += [(w_o_h, w_o), (w_g_h, w_g), (w_u_h, w_u), (w_d_h, w_d)]
     loads = [pltpu.make_async_copy(s, d, load.at[n]) for n, (s, d) in enumerate(moves)]
-    for item in loads:
+    loads[0].start()
+
+    normed = rms_scale(tok[...].astype(F32), gain_a[...].astype(F32).reshape(1, model_width)).astype(BF16)
+    loads[0].wait()
+    for item in loads[1:]:
         item.start()
-
-    normed = rms_scale(tok[...].astype(F32), gain_a[...].astype(F32)).astype(BF16)
-    loads[0].wait()
     queries[me] = swap_heads(dot(normed, w_q[...]), groups, per_group).astype(BF16)
     pl.semaphore_wait(barrier, count + exp_count - 2)
 
@@ -280,7 +281,7 @@
 
     for n in range(12, 16):
         loads[n].wait()
-    proj_out[...] = dot(attended, w_o[...])
+    proj_out[...] = dot(attended, w_o[...]).astype(BF16)
 
     def to_exp(j):
         there = lax.rem(col + j, exp_count)
@@ -290,29 +291,118 @@
         to_exp(j).start()
     for j in range(1, exp_count):
         to_exp(j).wait()
-    projected = proj_out[...]
+    projected = proj_out[...].astype(F32)
     for j in range(1, exp_count):
-        projected = projected + proj_in[j]
+        projected = projected + proj_in[j].astype(F32)
     mixed = tok[...].astype(F32) + projected
     mixed_buf[...] = mixed
-    rows_in[me] = rms_scale(mixed, gain_m[...].astype(F32)).astype(BF16)
-    gather_rows(rows_in, me, count, chip_s, chip_r, core_s, core_r)
+    chips = count // 2
+    chip, core = me // 2, lax.rem(me, 2)
+    partner = chip * 2 + (1 - core)
+    rows_in[core] = rms_scale(
+        mixed, gain_m[...].astype(F32).reshape(1, model_width)
+    ).astype(BF16)
+
+    def to_chip(k):
+        there = lax.rem(chip + k, chips) * 2 + core
+        return push(
+            rows_in.at[core], rows_in.at[k * 2 + core], chip_s.at[k], chip_r.at[k], {"pool": there}
+        )
+
+    def to_core(k):
+        held = rows_in.at[k * 2 + core]
+        return push(held, held, core_s.at[k], core_r.at[k], {"pool": partner})
+
+    def start_chip(k, carry):
+        to_chip(k).start()
+        return carry
+
+    lax.fori_loop(1, chips, start_chip, 0)
+    to_core(0).start()
 
     half = out.shape[1]
     cols = pl.ds(pl.multiple_of(col * half, half), half)
-    everyone = rows_in[...].reshape(count * rows, tok.shape[1])
-    gate_act = dot(everyone, w_g[...])
-    up_act = dot(everyone, w_u[...])
-    hidden = (gate_act / (1.0 + jnp.exp(-gate_act)) * up_act).astype(BF16)
-    made[...] = dot(hidden, w_d[:, cols]).astype(BF16).reshape(count, rows, half)
-    exchange(made, back, me, count, b_s, b_r)
-
-    def combine(e, total):
-        coeff = jnp.sum(jnp.where(ids[...] == e, gates[...], 0.0), axis=1, keepdims=True)
-        return total + coeff * back[e].astype(F32)
-
-    share = lax.fori_loop(0, count, combine, jnp.zeros((rows, half), F32))
-    out[...] = (mixed_buf[:, cols] + share).astype(BF16)
+
+    def give(i):
+        k, there_core = i // 2, lax.rem(i, 2)
+        there = lax.rem(chip - k + chips, chips) * 2 + there_core
+        return push(
+            made.at[i], back.at[me], b_s.at[i], b_r.at[k * 2 + core], {"pool": there}
+        )
+
+    def forward(k, carry):
+        to_chip(k).wait_recv()
+        to_core(k).start()
+        return carry
+
+    def finish_core(k, carry):
+        to_core(k).wait_recv()
+        return carry
+
+    def start_give(i, carry):
+        give(i).start()
+        return carry
+
+    near = chips // 2
+    for low, high in ((0, near), (near, chips)):
+        lax.fori_loop(max(low, 1), high, forward, 0)
+        lax.fori_loop(low, high, finish_core, 0)
+        some = rows_in[2 * low : 2 * high].reshape((high - low) * 2 * rows, model_width)
+        gate_act = dot(some, w_g[...])
+        up_act = dot(some, w_u[...])
+        hidden = (gate_act / (1.0 + jnp.exp(-gate_act)) * up_act).astype(BF16)
+        result = dot(hidden, w_d[:, cols]).astype(BF16)
+        made[2 * low : 2 * high] = result.reshape((high - low) * 2, rows, half)
+        if low == 0:
+            give(1 - core).start()
+        lax.fori_loop(2 * max(low, 1), 2 * high, start_give, 0)
+
+    eye_rows = iota((rows, rows), 0) == iota((rows, rows), 1)
+
+    def weigh(e, carry):
+        line = jnp.sum(jnp.where(ids[...] == e, gates[...], 0.0), axis=0, keepdims=True)
+        column = jnp.sum(jnp.where(eye_rows, line, 0.0), axis=1, keepdims=True)
+        coeff[e] = jnp.broadcast_to(column, (rows, LANES))
+        return carry
+
+    lax.fori_loop(0, count, weigh, 0)
+
+    def arrival(j):
+        k, from_core = j // 2, lax.rem(j, 2)
+        source = lax.rem(chip + k, chips) * 2 + from_core
+        return source, push(
+            made.at[0], back.at[source], b_s.at[j], b_r.at[j], {"pool": partner}
+        )
+
+    own = made[core].astype(F32) * coeff[me][:, 0:1]
+    total = mixed_buf[:, cols] + own
+    _, first = arrival(1 - core)
+    first.wait_recv()
+    total = total + coeff[partner][:, 0:1] * back[partner].astype(F32)
+
+    def combine(j, total):
+        source, copy = arrival(j)
+        copy.wait_recv()
+        return total + coeff[source][:, 0:1] * back[source].astype(F32)
+
+    out[...] = lax.fori_loop(2, count, combine, total).astype(BF16)
+
+    def drain_give(i, carry):
+        give(i).wait_send()
+        return carry
+
+    def drain_chip(k, carry):
+        to_chip(k).wait_send()
+        return carry
+
+    def drain_core(k, carry):
+        to_core(k).wait_send()
+        return carry
+
+    give(1 - core).wait_send()
+    lax.fori_loop(2, count, drain_give, 0)
+    lax.fori_loop(1, chips, drain_chip, 0)
+    lax.fori_loop(0, chips, drain_core, 0)
 
 
 def on_device(
@@ -358,12 +448,13 @@
             pltpu.VMEM((slot_count, LANES), F32),
             pltpu.VMEM((count, rows, width + LANES), BF16),
             pltpu.VMEM((count, rows, width + LANES), BF16),
-            pltpu.VMEM((rows, model_width), F32),
-            pltpu.VMEM((exp_count, rows, model_width), F32),
+            pltpu.VMEM((rows, model_width), BF16),
+            pltpu.VMEM((exp_count, rows, model_width), BF16),
             pltpu.VMEM((count, rows, model_width), BF16),
             pltpu.VMEM((rows, model_width), F32),
             pltpu.VMEM((count, rows, half), BF16),
             pltpu.VMEM((count, rows, half), BF16),
+            pltpu.VMEM((count, rows, LANES), F32),
             dma((16,)),
             dma((chips,)), dma((chips,)), dma((chips,)), dma((chips,)),
             dma((count,)), dma((count,)),
@@ -376,8 +467,8 @@
         ),
         name="layer",
     )(
-        tokens, norm_attn.reshape(1, -1), norm_moe.reshape(1, -1), block_table, lengths,
-        expert_ids, gate_weights, w_query, w_key, w_value, hidden_store, k_cache, v_cache,
+        tokens, norm_attn, norm_moe, block_table, lengths,
+        expert_ids.T, gate_weights.T, w_query, w_key, w_value, hidden_store, k_cache, v_cache,
         w_out, w_gate[0], w_up[0], w_down[0],
     )
 

time: 59.9 us -> 54.2 us (0.905); the launches traced: 58.8 us -> 53.9 us
  local copies, waits for them, and re-layouts: 6.57 us -> 1.32 us
    unnamed x3 -> x1, local copies, waits for them, and re-layouts: 4.02 us -> 1.32 us
    reshape x2 -> x0, local copies, waits for them, and re-layouts: 2.55 us -> none  [the longest x1 1.28 us: on_device(): norm_moe.reshape(1, -1)]
where the time goes in v3:
time: 54.2 us; the launch traced here: 53.9 us
  Pallas kernels  52.6 us (97%)
  local copies, waits for them, and re-layouts  1.32 us (2%)
    pallas_call x1, Pallas kernels, on_device(): pl.pallas_call(functools.partial(layer_kernel, count, exp_count, groups,...  52.6 us
    unnamed x1, local copies, waits for them, and re-layouts  1.32 us

profile of v3, /device:TPU:0, one launch (start us, length us, event | category | flops | bytes accessed | tf_op | source)
XLA Modules:
  0.0 53.9 jit_solution(14551185865196961878)
XLA Ops:
  0.0 52.6 %layer.1 = bf16[16,512]{1,0:T(8,128)(2,1)} custom-call(bf16[16,1024]{1,0:T(8,128)(2,1)} %tok.1, bf16[1024]{0:T(1024)(128)(2,1)} %gain_a.1, bf16[1024]{0:T(1024)(128)(2,1)} %gain_m.1, s32[256,128]{1,0:T(8,128)} %table.1, s32[256]{0:T(256)} %lengths.1, s32[8,16]{1,0:T(8,128)} %bitcast.8, f32[8,16]{1,0:T(8,128)} %bitcast.9, bf16[1024,512]{1,0:T(8,128)(2,1)} %w_q_h.1, ...), custom_call_target="tpu_custom_call" | custom-call | tf_op jit(solution)/shard_map/layer/pallas_call | solution.py:427
  52.6 1.3 %copy.19 = bf16[16,512]{1,0:T(8,128)(2,1)} copy(bf16[16,512]{1,0:T(8,128)(2,1)} %layer.1) | data formatting | bytes 32768

commit v4 on v3

--- a/solution.py
+++ b/solution.py
@@ -188,12 +188,16 @@
         for n in range(1, 4):
             loads[n].wait()
 
-        def one(n, carry):
-            keys[kept + n] = dot(hid[n], w_k[...]).astype(BF16)
-            values[kept + n] = dot(hid[n], w_v[...]).astype(BF16)
+        group = 8 if fresh % 8 == 0 else 1
+
+        def some(n, carry):
+            stored = hid[pl.ds(n * group, group)].reshape(group * page, model_width)
+            place = pl.ds(kept + n * group, group)
+            keys[place] = dot(stored, w_k[...]).astype(BF16).reshape(group, page, key_width)
+            values[place] = dot(stored, w_v[...]).astype(BF16).reshape(group, page, key_width)
             return carry
 
-        lax.fori_loop(0, fresh, one, 0)
+        lax.fori_loop(0, fresh // group, some, 0)
 
     gather_rows(queries, me, count, q_cs, q_cr, q_ps, q_pr, find_slots, project_hidden)
     for n in range(4, 12):

time: 54.2 us -> 51.7 us (0.954)
  Pallas kernels: 52.6 us -> 50.1 us
    pallas_call x1, Pallas kernels: 52.6 us -> 50.1 us  [on_device(): pl.pallas_call(functools.partial(layer_kernel, count, exp_count, groups,...]
where the time goes in v4:
time: 51.7 us; the launch traced here: 51.4 us
  Pallas kernels  50.1 us (97%)
  local copies, waits for them, and re-layouts  1.32 us (3%)
    pallas_call x1, Pallas kernels, on_device(): pl.pallas_call(functools.partial(layer_kernel, count, exp_count, groups,...  50.1 us
    unnamed x1, local copies, waits for them, and re-layouts  1.32 us

profile of v4, /device:TPU:0, one launch (start us, length us, event | category | flops | bytes accessed | tf_op | source)
XLA Modules:
  0.0 51.4 jit_solution(10821954408705351511)
XLA Ops:
  0.0 50.1 %layer.1 = bf16[16,512]{1,0:T(8,128)(2,1)} custom-call(bf16[16,1024]{1,0:T(8,128)(2,1)} %tok.1, bf16[1024]{0:T(1024)(128)(2,1)} %gain_a.1, bf16[1024]{0:T(1024)(128)(2,1)} %gain_m.1, s32[256,128]{1,0:T(8,128)} %table.1, s32[256]{0:T(256)} %lengths.1, s32[8,16]{1,0:T(8,128)} %bitcast.8, f32[8,16]{1,0:T(8,128)} %bitcast.9, bf16[1024,512]{1,0:T(8,128)(2,1)} %w_q_h.1, ...), custom_call_target="tpu_custom_call" | custom-call | tf_op jit(solution)/shard_map/layer/pallas_call | solution.py:431
  50.1 1.3 %copy.19 = bf16[16,512]{1,0:T(8,128)(2,1)} copy(bf16[16,512]{1,0:T(8,128)(2,1)} %layer.1) | data formatting | bytes 32768
